TPU v7x, 128 devices: a whole 4x4x4 slice. The times are simulated.
128 devices in a mesh: layer: 4 (over z_lo, core), latent: 32 (over x, z_hi, y).
Axes of the slice: x: 4, y: 4, z: 4 (z_hi: 2, z_lo: 2; z = z_hi * 2 + z_lo), core: 2. Of those that a mesh axis runs over, the one named last changes fastest.
Arguments:
- residuals: bfloat16 [4, 512, 3584], P('layer', 'latent'), may hold values from -6 to 6
- enc_weight: bfloat16 [4, 3584, 24576], P('layer', None, 'latent'), may hold values from -0.046875 to 0.046875
- dec_weight: bfloat16 [4, 24576, 3584], P('layer', 'latent'), may hold values from -0.0390625 to 0.0390625
- enc_bias: float32 [24576], P('latent'), may hold values from -1 to 0.5
- dec_bias: float32 [4, 3584], P('layer'), may hold values from -3 to 3
Outputs:
- enc_grad: bfloat16 [4, 3584, 24576], P('layer', None, 'latent')
- dec_grad: bfloat16 [4, 24576, 3584], P('layer', 'latent')
- enc_bias_grad: float32 [24576], P('latent')
All inputs are finite; a program needn't handle non-finite values.
Results may differ from a plain program's by a relative error of at most 0.02.
Values may be sent and summed in bfloat16 or wider, within the bound.
No kernel may reach another device: no remote copies, remote signals or barrier semaphores. Data moves between devices by JAX's collectives and lax.ppermute only.
A program may use at most 128 MiB of HBM per device.

v0:
```python
import jax
import jax.numpy as jnp
from jax import lax
from jax.sharding import PartitionSpec as P

sparsity_weight = 0.5
sharpness = 4.0


def per_device(residuals, enc_weight, dec_weight, enc_bias, dec_bias):
    own_rows = residuals[0]
    enc_local = enc_weight[0]
    dec_local = dec_weight[0]
    gathered = lax.all_gather(own_rows, "latent", axis=0, tiled=True)
    pre_part = jnp.dot(gathered, enc_local, preferred_element_type=jnp.float32)
    row_norms = jnp.sqrt(jnp.sum(jnp.square(dec_local.astype(jnp.float32)), axis=1) + 1e-06)
    pre_total, weight_sum = lax.psum((pre_part, row_norms), "layer")
    pre_full = pre_total + enc_bias[None, :]
    latents = (jax.nn.softplus(sharpness * pre_full) / sharpness).astype(jnp.bfloat16)
    gate_all = jax.nn.sigmoid(sharpness * pre_full)
    act_sum = jnp.sum(latents.astype(jnp.float32), axis=0)
    lat_rows = latents
    rebuilt = lax.psum_scatter(
        jnp.dot(lat_rows, dec_local, preferred_element_type=jnp.float32).astype(jnp.bfloat16),
        "latent",
        scatter_dimension=0,
        tiled=True,
    ).astype(jnp.float32)
    misfit = rebuilt + dec_bias[0][None, :] - own_rows.astype(jnp.float32)
    err_grad = (2.0 * misfit).astype(jnp.bfloat16)
    err_piece = lax.all_gather(err_grad, "latent", axis=0, tiled=True)
    lat_rows = latents
    dec_acc = lax.dot_general(
        lat_rows, err_piece, (((0,), (0,)), ((), ())), preferred_element_type=jnp.float32
    )
    back_rows = lax.dot_general(
        err_piece, dec_local, (((1,), (1,)), ((), ())), preferred_element_type=jnp.float32
    )
    lat_part = back_rows
    dec_acc, lat_part = (dec_acc, lat_part)
    penalty = sparsity_weight * weight_sum[None, :]
    lat_grad = lax.psum(lat_part.astype(jnp.bfloat16), "layer").astype(jnp.float32) + penalty
    pre_grad = (lat_grad * gate_all).astype(jnp.bfloat16)
    enc_grad = lax.dot_general(
        gathered, pre_grad, (((0,), (0,)), ((), ())), preferred_element_type=jnp.float32
    ).astype(jnp.bfloat16)
    enc_bias_grad = jnp.sum(pre_grad.astype(jnp.float32), axis=0)
    penalty_term = (
        sparsity_weight * act_sum[:, None] * dec_local.astype(jnp.float32) / row_norms[:, None]
    )
    dec_grad = (dec_acc + penalty_term).astype(jnp.bfloat16)
    return (enc_grad[None], dec_grad[None], enc_bias_grad)


def solution(mesh):
    in_specs = (
        P("layer", "latent", None),
        P("layer", None, "latent"),
        P("layer", "latent", None),
        P("latent"),
        P("layer", None),
    )
    out_specs = (P("layer", None, "latent"), P("layer", "latent", None), P("latent"))
    return jax.shard_map(
        per_device, mesh=mesh, in_specs=in_specs, out_specs=out_specs, check_vma=False
    )
```

profile of v0, /device:TPU:1, one launch (start us, length us, event | category | flops | bytes accessed | tf_op | source)
XLA Modules:
  0.0 496.8 jit_solution(12142019913235078704)
XLA Ops:
  7.2 0.0 all-gather.6.cloned.1.call-start
  7.2 0.7 all-gather.6.cloned.1.call-update
  7.9 0.0 copy-start.2
  7.9 0.0 all-reduce.3.cloned.1.call-start
  8.0 84.8 %all-gather.6.cloned.1.call-done = bf16[1,512,3584]{2,1,0:T(8,128)(2,1)} async-done(((bf16[1,16,3584]{2,1,0:T(8,128)(2,1)}), bf16[1,512,3584]{2,1,0:T(8,128)(2,1)}) %all-gather.6.cloned.1.call-update) | async-done | bytes 3670032 | tf_op jit(solution)/shard_map/all_gather | solution.py:14
  92.7 7.8 %fusion.9 = f32[512,768]{1,0:T(8,128)} fusion(bf16[1,3584,768]{2,1,0:T(8,128)(2,1)} %param.6, bf16[1,512,3584]{2,1,0:T(8,128)(2,1)} %all-gather.6.cloned.1.call-done), kind=kOutput, calls=%fused_computation.13 | convolution fusion | flops 2818572288 | bytes 10747904 | tf_op jit(solution)/shard_map/dot_general | solution.py:15
  100.6 0.0 all-reduce.3.cloned.1.call-update
  100.6 0.0 reduce-scatter.2.cloned.1.call-start
  100.6 47.8 %all-reduce.3.cloned.1.call-done = f32[512,768]{1,0:T(8,128)} async-done(((f32[512,768]{1,0:T(8,128)}), f32[512,768]{1,0:T(8,128)}) %all-reduce.3.cloned.1.call-update) | async-done | bytes 1572880 | tf_op jit(solution)/shard_map/psum | solution.py:17
  148.5 0.0 copy-done.2
  148.5 2.6 convert_reduce_fusion.1
  151.0 7.0 %convolution_convert_fusion.1 = bf16[512,3584]{1,0:T(8,128)(2,1)} fusion(bf16[512,768]{1,0:T(8,128)(2,1)S(1)} %get-tuple-element.9, bf16[1,768,3584]{2,1,0:T(8,128)(2,1)} %param.7), kind=kOutput, calls=%fused_computation.9 | convolution fusion | flops 2820407296 | bytes 9961472 | tf_op jit(solution)/shard_map/dot_general | solution.py:24
  158.1 0.0 reduce-scatter.2.cloned.1.call-update
  158.1 0.0 all-gather.4.cloned.1.call-start
  158.1 0.6 copy-done.3
  158.8 168.0 %reduce-scatter.2.cloned.1.call-done = bf16[16,3584]{1,0:T(8,128)(2,1)} async-done(((bf16[512,3584]{1,0:T(8,128)(2,1)}), bf16[16,3584]{1,0:T(8,128)(2,1)}) %reduce-scatter.2.cloned.1.call-update) | async-done | bytes 114704 | tf_op jit(solution)/shard_map/reduce_scatter | solution.py:23
  326.8 0.0 copy-done.1
  326.8 1.6 fusion.19
  328.4 0.0 all-gather.4.cloned.1.call-update
  328.4 0.0 all-reduce.5.cloned.1.call-start
  328.5 3.7 fusion
  332.2 28.6 %psum.23 = f32[768]{0:T(1024)S(1)} all-reduce(f32[768]{0:T(1024)S(1)} %add_sqrt_fusion), channel_id=1, replica_groups=mesh['layer'=4,'latent'=32] {'layer'}, use_global_device_ids=true, to_apply=%region_4.5 | all-reduce | flops 768 | bytes 6144 | tf_op jit(solution)/shard_map/psum | solution.py:17
  360.8 66.0 %all-gather.4.cloned.1.call-done = bf16[512,3584]{1,0:T(8,128)(2,1)} async-done(((bf16[16,3584]{1,0:T(8,128)(2,1)}), bf16[512,3584]{1,0:T(8,128)(2,1)}) %all-gather.4.cloned.1.call-update) | async-done | bytes 3670032 | tf_op jit(solution)/shard_map/all_gather | solution.py:31
  426.8 7.6 %fusion.15 = bf16[512,768]{1,0:T(8,128)(2,1)} fusion(bf16[512,3584]{1,0:T(8,128)(2,1)} %all-gather.4.cloned.1.call-done, bf16[1,768,3584]{2,1,0:T(8,128)(2,1)} %param.7), kind=kOutput, calls=%fused_computation.24 | convolution fusion | flops 2818965504 | bytes 9961472 | tf_op jit(solution)/shard_map/dot_general | solution.py:36
  434.4 0.0 all-reduce.5.cloned.1.call-update
  434.4 0.0 copy-start
  434.4 8.4 %fusion.4 = bf16[1,768,3584]{2,1,0:T(8,128)(2,1)} fusion(bf16[512,768]{1,0:T(8,128)(2,1)S(1)} %get-tuple-element.9, bf16[512,3584]{1,0:T(8,128)(2,1)} %all-gather.4.cloned.1.call-done, bf16[1,768,3584]{2,1,0:T(8,128)(2,1)} %param.7, f32[768]{0:T(1024)S(1)} %add_sqrt_fusion, f32[768]{0:T(1024)S(1)} %broadcast_multiply_fusion), kind=kOutput, calls=%fused_computation.7 | convolution fusion | flops 2832334848 | bytes 15472640 | tf_op jit(solution)/shard_map/dot_general | solution.py:33
  442.9 29.9 %all-reduce.5.cloned.1.call-done = bf16[512,768]{1,0:T(8,128)(2,1)} async-done(((bf16[512,768]{1,0:T(8,128)(2,1)}), bf16[512,768]{1,0:T(8,128)(2,1)}) %all-reduce.5.cloned.1.call-update) | async-done | bytes 786448 | tf_op jit(solution)/shard_map/psum | solution.py:42
  472.8 0.0 copy-done
  472.8 2.3 convert_reduce_fusion
  475.1 6.9 %fusion.5 = bf16[1,3584,768]{1,2,0:T(8,128)(2,1)} fusion(bf16[512,768]{1,0:T(8,128)(2,1)S(1)} %get-tuple-element.7, bf16[1,512,3584]{2,1,0:T(8,128)(2,1)} %all-gather.6.cloned.1.call-done), kind=kOutput, calls=%fused_computation.8 | convolution fusion | flops 2821324800 | bytes 9961472 | tf_op jit(solution)/shard_map/dot_general | solution.py:44
  482.0 8.3 %copy.8 = bf16[1,3584,768]{2,1,0:T(8,128)(2,1)} copy(bf16[1,3584,768]{1,2,0:T(8,128)(2,1)} %fusion.5) | data formatting | bytes 11010048
  (6 shorter events, 0.1 us)
Async XLA Ops:
  7.2 85.6 %all-gather.6.cloned.1.call-start = ((), (), s32[]{:S(2)}) async-start(), calls=%async_computation.5 | async-start | bytes 3784704 | tf_op jit(solution)/shard_map/all_gather | solution.py:14
  7.9 140.6 %copy-start.2 = (f32[768]{0:T(1024)S(1)}, f32[768]{0:T(1024)}, u32[]{:S(2)}) copy-start(f32[768]{0:T(1024)} %param.8) | copy-start | bytes 9220
  7.9 140.6 %all-reduce.3.cloned.1.call-start = ((), (), s32[]{:S(2)}) async-start(), calls=%async_computation.1 | async-start | bytes 3145728 | tf_op jit(solution)/shard_map/psum | solution.py:17
  100.6 226.2 %reduce-scatter.2.cloned.1.call-start = ((), (), s32[]{:S(2)}) async-start(), calls=%async_computation.2 | async-start | bytes 3784704 | tf_op jit(solution)/shard_map/reduce_scatter | solution.py:23
  158.1 0.7 copy-start.3
  158.1 168.8 %copy-start.1 = (bf16[1,16,3584]{2,1,0:T(8,128)(2,1)S(1)}, bf16[1,16,3584]{2,1,0:T(8,128)(2,1)}, u32[]{:S(2)}) copy-start(bf16[1,16,3584]{2,1,0:T(8,128)(2,1)} %param.5) | copy-start | bytes 344068
  158.1 268.7 %all-gather.4.cloned.1.call-start = ((), (), s32[]{:S(2)}) async-start(), calls=%async_computation.3 | async-start | bytes 3784704 | tf_op jit(solution)/shard_map/all_gather | solution.py:31
  328.4 144.4 %all-reduce.5.cloned.1.call-start = ((), (), s32[]{:S(2)}) async-start(), calls=%async_computation.4 | async-start | bytes 1572864 | tf_op jit(solution)/shard_map/psum | solution.py:42
  434.4 38.4 %copy-start = (f32[512,768]{1,0:T(8,128)S(1)}, f32[512,768]{1,0:T(8,128)}, u32[]{:S(2)}) copy-start(f32[512,768]{1,0:T(8,128)} %all-reduce.3.cloned.1.call-done) | copy-start | bytes 4718596
Sparse Core Ops, SparseCore 0:
  11.0 81.7 all-gather.5
  100.7 47.7 all-reduce.2
  158.2 168.5 reduce-scatter.1
  330.7 96.1 all-gather.3
  434.6 38.1 all-reduce.4
where the time goes:
time: 497 us
  waiting for transfers between devices  397 us (80%)
  matrix products  37.7 us (8%)
  blocking collectives  28.6 us (6%)
  between operations  13.8 us (3%)
  other arithmetic  10.2 us (2%)
  local copies, waits for them, and re-layouts  8.91 us (2%)
    reduce_scatter x1, waiting for transfers between devices, per_device(): lax.psum_scatter(jnp.dot(lat_rows, dec_local, preferred_element_type=jnp....  168 us
    all_gather x1, waiting for transfers between devices, per_device(): gathered = lax.all_gather(own_rows, 'latent', axis=0, tiled=True)  84.8 us
    all_gather x1, waiting for transfers between devices, per_device(): err_piece = lax.all_gather(err_grad, 'latent', axis=0, tiled=True)  66 us
    psum x1, waiting for transfers between devices, per_device(): pre_total, weight_sum = lax.psum((pre_part, row_norms), 'layer')  47.8 us
    psum x1, waiting for transfers between devices, per_device(): lax.psum(lat_part.astype(jnp.bfloat16), 'layer').astype(jnp.float32)  29.9 us
    psum x1, blocking collectives, per_device(): pre_total, weight_sum = lax.psum((pre_part, row_norms), 'layer')  28.6 us
  transfers between devices with their start and end apart: 5, of which 5 were waited for; matrix products, arithmetic and copies ran while one was open for 2% of the time, Pallas kernels for 0%

commit v1 on v0

--- a/solution.py
+++ b/solution.py
@@ -1,3 +1,4 @@
+import functools
 import jax
 import jax.numpy as jnp
 from jax import lax
@@ -7,11 +8,21 @@
 sharpness = 4.0
 
 
+def push_view_on(mine, out_dim):
+    current_arr = jax.lax.all_to_all(
+        jnp.stack([mine for _ in range(jax.lax.axis_size("latent"))]), "latent", 0, 0
+    )
+    return jnp.concatenate(current_arr, axis=out_dim)
+
+
+proceed_rates = functools.partial(push_view_on, out_dim=0)
+
+
 def per_device(residuals, enc_weight, dec_weight, enc_bias, dec_bias):
     own_rows = residuals[0]
     enc_local = enc_weight[0]
     dec_local = dec_weight[0]
-    gathered = lax.all_gather(own_rows, "latent", axis=0, tiled=True)
+    gathered = proceed_rates(own_rows)
     pre_part = jnp.dot(gathered, enc_local, preferred_element_type=jnp.float32)
     row_norms = jnp.sqrt(jnp.sum(jnp.square(dec_local.astype(jnp.float32)), axis=1) + 1e-06)
     pre_total, weight_sum = lax.psum((pre_part, row_norms), "layer")

time: 497 us -> 467 us (0.940)
  waiting for transfers between devices: 397 us -> 312 us
  blocking collectives: 28.6 us -> 84.8 us
    all_gather x1 -> x0, waiting for transfers between devices: 84.8 us -> none  [per_device(): gathered = lax.all_gather(own_rows, 'latent', axis=0, tiled=True)]
    all_to_all x0 -> x1, blocking collectives: none -> 56.2 us  [push_view_on(): jax.lax.all_to_all(jnp.stack([mine for _ in range(jax.lax.axis_size('late...]
    unnamed x9 -> x13, local copies, waits for them, and re-layouts: 8.91 us -> 10.8 us
  transfers between devices with their start and end apart: 5 -> 4, of which waited for: 5 -> 4; matrix products, arithmetic and copies ran while one was open for 2% -> 3% of each run, Pallas kernels for 0% -> 0%
where the time goes in v1:
time: 467 us
  waiting for transfers between devices  312 us (67%)
  blocking collectives  84.8 us (18%)
  matrix products  34 us (7%)
  between operations  13.8 us (3%)
  local copies, waits for them, and re-layouts  12.1 us (3%)
  other arithmetic  10.2 us (2%)
    reduce_scatter x1, waiting for transfers between devices, per_device(): lax.psum_scatter(jnp.dot(lat_rows, dec_local, preferred_element_type=jnp....  168 us
    all_gather x1, waiting for transfers between devices, per_device(): err_piece = lax.all_gather(err_grad, 'latent', axis=0, tiled=True)  66.2 us
    all_to_all x1, blocking collectives, push_view_on(): jax.lax.all_to_all(jnp.stack([mine for _ in range(jax.lax.axis_size('late...  56.2 us
    psum x1, waiting for transfers between devices, per_device(): pre_total, weight_sum = lax.psum((pre_part, row_norms), 'layer')  47.5 us
    psum x1, waiting for transfers between devices, per_device(): lax.psum(lat_part.astype(jnp.bfloat16), 'layer').astype(jnp.float32)  30 us
    psum x1, blocking collectives, per_device(): pre_total, weight_sum = lax.psum((pre_part, row_norms), 'layer')  28.6 us
    unnamed x13, local copies, waits for them, and re-layouts  10.8 us
  transfers between devices with their start and end apart: 4, of which 4 were waited for; matrix products, arithmetic and copies ran while one was open for 3% of the time, Pallas kernels for 0%

profile of v1, /device:TPU:1, one launch (start us, length us, event | category | flops | bytes accessed | tf_op | source)
XLA Modules:
  0.0 466.7 jit_solution(15551952564110971701)
XLA Ops:
  7.2 0.0 all-reduce.3.cloned.1.call-start
  7.2 1.3 stack.3
  8.5 0.0 copy-start.5
  8.5 56.2 %all_to_all.5 = bf16[32,16,3584]{2,1,0:T(8,128)(2,1)S(1)} all-to-all(bf16[32,16,3584]{2,1,0:T(8,128)(2,1)S(1)} %stack.3), channel_id=1, replica_groups=mesh['layer'=4,'latent'=32] {'latent'}, dimensions={0} | all-to-all | bytes 7340032 | tf_op jit(solution)/shard_map/all_to_all | solution.py:12
  64.7 1.8 copy-done.1
  66.5 0.0 copy-done.5
  66.6 4.1 fusion.9
  70.7 0.0 all-reduce.3.cloned.1.call-update
  70.7 0.0 reduce-scatter.2.cloned.1.call-start
  70.8 47.5 %all-reduce.3.cloned.1.call-done = f32[512,768]{1,0:T(8,128)} async-done(((f32[512,768]{1,0:T(8,128)}), f32[512,768]{1,0:T(8,128)}) %all-reduce.3.cloned.1.call-update) | async-done | bytes 1572880 | tf_op jit(solution)/shard_map/psum | solution.py:28
  118.2 0.0 copy-done.3
  118.2 2.6 convert_reduce_fusion.1
  120.8 7.0 %convolution_convert_fusion.1 = bf16[512,3584]{1,0:T(8,128)(2,1)} fusion(bf16[512,768]{1,0:T(8,128)(2,1)S(1)} %get-tuple-element.9, bf16[1,768,3584]{2,1,0:T(8,128)(2,1)} %param.7), kind=kOutput, calls=%fused_computation.9 | convolution fusion | flops 2820407296 | bytes 9961472 | tf_op jit(solution)/shard_map/dot_general | solution.py:35
  127.8 0.0 reduce-scatter.2.cloned.1.call-update
  127.8 0.0 all-gather.2.cloned.1.call-start
  127.9 0.6 copy-done.4
  128.5 168.0 %reduce-scatter.2.cloned.1.call-done = bf16[16,3584]{1,0:T(8,128)(2,1)} async-done(((bf16[512,3584]{1,0:T(8,128)(2,1)}), bf16[16,3584]{1,0:T(8,128)(2,1)}) %reduce-scatter.2.cloned.1.call-update) | async-done | bytes 114704 | tf_op jit(solution)/shard_map/reduce_scatter | solution.py:34
  296.6 0.0 copy-done.2
  296.6 1.6 multiply_convert_fusion.1
  298.2 0.0 all-gather.2.cloned.1.call-update
  298.2 0.0 all-reduce.5.cloned.1.call-start
  298.2 3.7 fusion
  301.9 28.6 %psum.23 = f32[768]{0:T(1024)S(1)} all-reduce(f32[768]{0:T(1024)S(1)} %add_sqrt_fusion), channel_id=1, replica_groups=mesh['layer'=4,'latent'=32] {'layer'}, use_global_device_ids=true, to_apply=%region_4.5 | all-reduce | flops 768 | bytes 6144 | tf_op jit(solution)/shard_map/psum | solution.py:28
  330.5 66.2 %all-gather.2.cloned.1.call-done = bf16[512,3584]{1,0:T(8,128)(2,1)} async-done(((bf16[16,3584]{1,0:T(8,128)(2,1)}), bf16[512,3584]{1,0:T(8,128)(2,1)}) %all-gather.2.cloned.1.call-update) | async-done | bytes 3670032 | tf_op jit(solution)/shard_map/all_gather | solution.py:42
  396.7 7.6 %fusion.13 = bf16[512,768]{1,0:T(8,128)(2,1)} fusion(bf16[512,3584]{1,0:T(8,128)(2,1)} %all-gather.2.cloned.1.call-done, bf16[1,768,3584]{2,1,0:T(8,128)(2,1)} %param.7), kind=kOutput, calls=%fused_computation.22 | convolution fusion | flops 2818965504 | bytes 9961472 | tf_op jit(solution)/shard_map/dot_general | solution.py:47
  404.3 0.0 all-reduce.5.cloned.1.call-update
  404.4 8.4 %fusion.4 = bf16[1,768,3584]{2,1,0:T(8,128)(2,1)} fusion(bf16[512,768]{1,0:T(8,128)(2,1)S(1)} %get-tuple-element.9, bf16[512,3584]{1,0:T(8,128)(2,1)} %all-gather.2.cloned.1.call-done, bf16[1,768,3584]{2,1,0:T(8,128)(2,1)} %param.7, f32[768]{0:T(1024)S(1)} %add_sqrt_fusion, f32[768]{0:T(1024)S(1)} %broadcast_multiply_fusion), kind=kOutput, calls=%fused_computation.7 | convolution fusion | flops 2832334848 | bytes 15472640 | tf_op jit(solution)/shard_map/dot_general | solution.py:44
  412.8 30.0 %all-reduce.5.cloned.1.call-done = bf16[512,768]{1,0:T(8,128)(2,1)} async-done(((bf16[512,768]{1,0:T(8,128)(2,1)}), bf16[512,768]{1,0:T(8,128)(2,1)}) %all-reduce.5.cloned.1.call-update) | async-done | bytes 786448 | tf_op jit(solution)/shard_map/psum | solution.py:53
  442.8 0.0 copy-done
  442.8 2.3 convert_reduce_fusion
  445.0 6.9 %fusion.5 = bf16[1,3584,768]{1,2,0:T(8,128)(2,1)} fusion(bf16[512,768]{1,0:T(8,128)(2,1)S(1)} %get-tuple-element.7, bf16[512,3584]{1,0:T(8,128)(2,1)} %bitcast.29), kind=kOutput, calls=%fused_computation.8 | convolution fusion | flops 2821324800 | bytes 9961472 | tf_op jit(solution)/shard_map/dot_general | solution.py:55
  451.9 8.3 %copy.8 = bf16[1,3584,768]{2,1,0:T(8,128)(2,1)} copy(bf16[1,3584,768]{1,2,0:T(8,128)(2,1)} %fusion.5) | data formatting | bytes 11010048
  (9 shorter events, 0.1 us)
Async XLA Ops:
  7.2 111.1 %all-reduce.3.cloned.1.call-start = ((), (), s32[]{:S(2)}) async-start(), calls=%async_computation.2 | async-start | bytes 3145728 | tf_op jit(solution)/shard_map/psum | solution.py:28
  8.5 58.0 %copy-start.5 = (bf16[1,3584,768]{2,1,0:T(8,128)(2,1)S(1)}, bf16[1,3584,768]{2,1,0:T(8,128)(2,1)}, u32[]{:S(2)}) copy-start(bf16[1,3584,768]{2,1,0:T(8,128)(2,1)} %param.6) | copy-start | bytes 16515076
  64.7 1.8 copy-start.1
  66.5 51.7 %copy-start.3 = (f32[768]{0:T(1024)S(1)}, f32[768]{0:T(1024)}, u32[]{:S(2)}) copy-start(f32[768]{0:T(1024)} %param.8) | copy-start | bytes 9220
  70.7 225.8 %reduce-scatter.2.cloned.1.call-start = ((), (), s32[]{:S(2)}) async-start(), calls=%async_computation.3 | async-start | bytes 3784704 | tf_op jit(solution)/shard_map/reduce_scatter | solution.py:34
  127.8 0.7 copy-start.4
  127.8 168.8 %copy-start.2 = (bf16[1,16,3584]{2,1,0:T(8,128)(2,1)S(1)}, bf16[1,16,3584]{2,1,0:T(8,128)(2,1)}, u32[]{:S(2)}) copy-start(bf16[1,16,3584]{2,1,0:T(8,128)(2,1)} %param.5) | copy-start | bytes 344068
  127.8 268.9 %all-gather.2.cloned.1.call-start = ((), (), s32[]{:S(2)}) async-start(), calls=%async_computation.4 | async-start | bytes 3784704 | tf_op jit(solution)/shard_map/all_gather | solution.py:42
  298.2 144.6 %all-reduce.5.cloned.1.call-start = ((), (), s32[]{:S(2)}) async-start(), calls=%async_computation.5 | async-start | bytes 1572864 | tf_op jit(solution)/shard_map/psum | solution.py:53
  404.3 38.4 %copy-start = (f32[512,768]{1,0:T(8,128)S(1)}, f32[512,768]{1,0:T(8,128)}, u32[]{:S(2)}) copy-start(f32[512,768]{1,0:T(8,128)} %all-reduce.3.cloned.1.call-done) | copy-start | bytes 4718596
Sparse Core Ops, SparseCore 0:
  70.8 47.3 all-reduce.2
  127.9 168.5 reduce-scatter.1
  300.5 96.1 all-gather.1
  404.5 38.2 all-reduce.4
